TPU v7x, 256 devices: a whole 4x4x8 slice. The times are simulated.
256 devices in a mesh: fsdp: 64 (over z_lo, y, x, core), dp: 4 (over z_hi).
Axes of the slice: x: 4, y: 4, z: 8 (z_hi: 4, z_lo: 2; z = z_hi * 2 + z_lo), core: 2. Of those that a mesh axis runs over, the one named last changes fastest.
Arguments:
- inputs: bfloat16 [4, 8192, 2560], P('dp', 'fsdp'), may hold values from -16 to 16
- up_weight: bfloat16 [2560, 6912], P('fsdp', 'dp'), may hold values from -0.125 to 0.125
- out_grad: bfloat16 [4, 8192, 6912], P(None, 'fsdp', 'dp'), may hold values from -6 to 6
Outputs:
- outputs: bfloat16 [4, 8192, 6912], P(None, 'fsdp', 'dp')
- in_grad: bfloat16 [4, 8192, 2560], P('dp', 'fsdp')
- up_grad: float32 [2560, 6912], P('fsdp', 'dp')
All inputs are finite; a program needn't handle non-finite values.
Results may differ from a plain program's by a relative error of at most 0.013.
Values may be sent and summed in bfloat16 or wider, within the bound.
A program may use at most 128 MiB of HBM per device.

v0:
```python
import jax
import jax.numpy as jnp
from jax import lax
from jax.sharding import PartitionSpec as P


def gelu_tanh(value):
    return jax.nn.gelu(value, approximate=True)


def times_transposed(left, right):
    return lax.dot_general(
        left, right, (((1,), (1,)), ((), ())), preferred_element_type=jnp.float32
    )


def on_device(inputs, up_weight, out_grad):
    all_clips = lax.all_gather(inputs, "dp", axis=0, tiled=True)
    clip_count, tok_count, width = all_clips.shape
    units = up_weight.shape[1]
    tok_rows = all_clips.reshape(clip_count * tok_count, width)
    grad_rows = out_grad.reshape(clip_count * tok_count, units)
    up_whole = lax.all_gather(up_weight, "fsdp", axis=0, tiled=True)
    pre = jnp.dot(tok_rows, up_whole, preferred_element_type=jnp.float32)
    outputs = gelu_tanh(pre).astype(jnp.bfloat16)
    pre_grad = jax.vjp(gelu_tanh, pre)[1](grad_rows.astype(jnp.float32))[0].astype(jnp.bfloat16)
    factor = 1.0 / jnp.sqrt(jnp.float32(clip_count * tok_count * lax.axis_size("fsdp")))
    partial_rows = times_transposed(pre_grad, up_whole).reshape(clip_count, tok_count, width)
    in_grad = lax.psum_scatter(
        partial_rows.astype(jnp.bfloat16), "dp", scatter_dimension=0, tiled=True
    )
    up_grad = lax.psum_scatter(
        lax.dot_general(
            tok_rows, pre_grad, (((0,), (0,)), ((), ())), preferred_element_type=jnp.float32
        )
        * factor,
        "fsdp",
        scatter_dimension=0,
        tiled=True,
    )
    outputs = outputs.reshape(clip_count, tok_count, units)
    return (outputs, in_grad, up_grad)


def solution(mesh):
    in_specs = (P("dp", "fsdp", None), P("fsdp", "dp"), P(None, "fsdp", "dp"))
    out_specs = (P(None, "fsdp", "dp"), P("dp", "fsdp", None), P("fsdp", "dp"))
    return jax.shard_map(
        on_device, mesh=mesh, in_specs=in_specs, out_specs=out_specs, check_vma=False
    )
```

profile of v0, /device:TPU:1, one launch (start us, length us, event | category | flops | bytes accessed | tf_op | source)
XLA Modules:
  0.0 585.7 jit_solution(14193802297332978485)
XLA Ops:
  7.2 0.0 all-gather.3.cloned.1.call-start
  7.2 0.7 all-gather.3.cloned.1.call-update
  7.9 0.0 all-gather.5.cloned.1.call-start
  7.9 0.7 all-gather.5.cloned.1.call-update
  8.6 0.0 reduce-scatter.5.cloned.1.call-start
  8.7 65.3 %all-gather.3.cloned.1.call-done = bf16[4,128,2560]{2,1,0:T(8,128)(2,1)} async-done(((bf16[1,128,2560]{2,1,0:T(8,128)(2,1)}), bf16[4,128,2560]{2,1,0:T(8,128)(2,1)}) %all-gather.3.cloned.1.call-update) | async-done | bytes 2621456 | tf_op jit(solution)/shard_map/all_gather | solution.py:18
  74.0 115.6 %all-gather.5.cloned.1.call-done = bf16[2560,1728]{1,0:T(8,128)(2,1)} async-done(((bf16[40,1728]{1,0:T(8,128)(2,1)}), bf16[2560,1728]{1,0:T(8,128)(2,1)}) %all-gather.5.cloned.1.call-update) | async-done | bytes 8847376 | tf_op jit(solution)/shard_map/all_gather | solution.py:23
  189.6 0.0 copy-start
  189.6 12.4 %fusion.6 = (bf16[512,1728]{0,1:T(8,128)(2,1)S(1)}, bf16[216,4,8,128]{3,2,1,0:T(8,128)(2,1)S(1)}) fusion(bf16[512,2560]{1,0:T(8,128)(2,1)} %bitcast.34, bf16[2560,1728]{1,0:T(8,128)(2,1)} %all-gather.5.cloned.1.call-done, bf16[4,128,1728]{1,2,0:T(8,128)(2,1)} %param.5), kind=kOutput, calls=%fused_computation.10 | convolution fusion | flops 4550197248 | bytes 16777216 | tf_op jit(solution)/shard_map/dot_general | solution.py:24
  202.0 0.0 copy-done
  202.0 6.4 %convolution_convert_fusion = bf16[512,2560]{1,0:T(8,128)(2,1)} fusion(bf16[512,1728]{0,1:T(8,128)(2,1)S(1)} %get-tuple-element.9, bf16[2560,1728]{1,0:T(8,128)(2,1)S(1)} %copy-done), kind=kOutput, calls=%fused_computation.3 | convolution fusion | flops 4531159040 | bytes 13238272 | tf_op jit(solution)/shard_map/dot_general | solution.py:12
  208.4 0.0 reduce-scatter.5.cloned.1.call-update
  208.4 0.2 reduce-scatter.7.cloned.1.call-start
  208.7 10.5 %multiply_bitcast_fusion = f32[2560,1728]{0,1:T(8,128)} fusion(bf16[512,1728]{0,1:T(8,128)(2,1)S(1)} %get-tuple-element.9, bf16[512,2560]{1,0:T(8,128)(2,1)} %bitcast.35), kind=kOutput, calls=%fused_computation | convolution fusion | flops 4534272000 | bytes 22085632 | tf_op jit(solution)/shard_map/dot_general | solution.py:33
  219.2 19.1 %copy.12 = f32[2560,1728]{1,0:T(8,128)} copy(f32[2560,1728]{0,1:T(8,128)} %multiply_bitcast_fusion) | data formatting | bytes 35389440
  238.3 0.0 reduce-scatter.7.cloned.1.call-update
  238.3 1.5 copy.18
  239.8 26.5 %reduce-scatter.5.cloned.1.call-done = bf16[1,128,2560]{2,1,0:T(8,128)(2,1)} async-done(((bf16[4,128,2560]{2,1,0:T(8,128)(2,1)}), bf16[1,128,2560]{2,1,0:T(8,128)(2,1)}) %reduce-scatter.5.cloned.1.call-update) | async-done | bytes 655376 | tf_op jit(solution)/shard_map/reduce_scatter | solution.py:29
  266.3 312.8 %reduce-scatter.7.cloned.1.call-done = f32[40,1728]{1,0:T(8,128)} async-done(((f32[2560,1728]{1,0:T(8,128)}), f32[40,1728]{1,0:T(8,128)}) %reduce-scatter.7.cloned.1.call-update) | async-done | bytes 276496
Async XLA Ops:
  7.2 66.8 %all-gather.3.cloned.1.call-start = ((), (), s32[]{:S(2)}) async-start(), calls=%async_computation.2 | async-start | bytes 3276800 | tf_op jit(solution)/shard_map/all_gather | solution.py:18
  7.9 181.7 %all-gather.5.cloned.1.call-start = ((), (), s32[]{:S(2)}) async-start(), calls=%async_computation.3 | async-start | bytes 9318400 | tf_op jit(solution)/shard_map/all_gather | solution.py:23
  8.6 257.6 %reduce-scatter.5.cloned.1.call-start = ((), (), s32[]{:S(2)}) async-start(), calls=%async_computation.4 | async-start | bytes 3276800 | tf_op jit(solution)/shard_map/reduce_scatter | solution.py:29
  189.6 12.4 %copy-start = (bf16[2560,1728]{1,0:T(8,128)(2,1)S(1)}, bf16[2560,1728]{1,0:T(8,128)(2,1)}, u32[]{:S(2)}) copy-start(bf16[2560,1728]{1,0:T(8,128)(2,1)} %all-gather.5.cloned.1.call-done) | copy-start | bytes 26542084
  208.4 370.7 %reduce-scatter.7.cloned.1.call-start = ((), (), s32[]{:S(2)}) async-start(), calls=%async_computation.5 | async-start | bytes 18636800
Sparse Core Ops, SparseCore 0:
  9.8 64.1 all-gather.2
  75.8 113.7 all-gather.4
  208.5 57.6 reduce-scatter.4
  269.3 309.8 reduce-scatter.6
where the time goes:
time: 591 us; the launch traced here: 586 us
  waiting for transfers between devices  522 us (88%)
  matrix products  29.3 us (5%)
  local copies, waits for them, and re-layouts  20.6 us (3%)
  between operations  13.8 us (2%)
    unnamed x5, waiting for transfers between devices  314 us
    all_gather x1, waiting for transfers between devices, on_device(): up_whole = lax.all_gather(up_weight, 'fsdp', axis=0, tiled=True)  116 us
    all_gather x1, waiting for transfers between devices, on_device(): all_clips = lax.all_gather(inputs, 'dp', axis=0, tiled=True)  65.3 us
    reduce_scatter x1, waiting for transfers between devices, on_device(): lax.psum_scatter(partial_rows.astype(jnp.bfloat16), 'dp', scatter_dimensi...  26.5 us
    unnamed x3, local copies, waits for them, and re-layouts  19.1 us
    dot_general x1, matrix products, on_device(): pre = jnp.dot(tok_rows, up_whole, preferred_element_type=jnp.float32)  12.4 us
  transfers between devices with their start and end apart: 4, of which 4 were waited for; matrix products, arithmetic and copies ran while one was open for 5% of the time, Pallas kernels for 0%

commit v1 on v0

v1 whole, which is shorter than its diff:
```python
import functools

import jax
import jax.numpy as jnp
from jax import lax
from jax.experimental import pallas as pl
from jax.experimental.pallas import tpu as pltpu
from jax.sharding import PartitionSpec as P

MESH = pl.DeviceIdType.MESH
F32, BF16 = jnp.float32, jnp.bfloat16
SIDE = 4
TILE = 256
CHUNK = 64


def place(device):
    return {"fsdp": device[0], "dp": device[1]}


def remote(src, dst, send_sem, recv_sem, device):
    return pltpu.make_async_remote_copy(
        src_ref=src, dst_ref=dst, send_sem=send_sem, recv_sem=recv_sem,
        device_id=place(device), device_id_type=MESH,
    )


def gelu_pair(v):
    c = 0.7978845608028654
    sq = v * v
    t = jnp.tanh(v * (c + (c * 0.044715) * sq))
    half = 0.5 * (1.0 + t)
    slope = half + (0.5 * v) * (1.0 - t * t) * (c + (3.0 * c * 0.044715) * sq)
    return v * half, slope


def kernel(
    factor, x_hbm, w_ref, gt_hbm, out_hbm, ing_hbm, dw_ref,
    xall, xt, wfull, wst, gt, g, pg, outn, outt, pre, psend, zr1, zr2, ing,
    lhs, ssend, srecv, dsend, r1, r2, r3, d4, r4, fin,
    send_sem, w_sem, x_sem, z1_sem, z2_sem, s_sem, r_sem, local_sem,
):
    fs, p = lax.axis_index("fsdp"), lax.axis_index("dp")
    k = lax.rem(fs, 2)
    x = lax.rem(lax.div(fs, 2), SIDE)
    y = lax.rem(lax.div(fs, 2 * SIDE), SIDE)
    l = lax.div(fs, 2 * SIDE * SIDE)
    home = k == l
    a = x * (1 - k) + y * k
    b = y * (1 - k) + x * k
    toks = xall.shape[1]
    half_toks = toks // 2
    rows = wfull.shape[2]
    width = wfull.shape[3]
    units = w_ref.shape[1]
    tiles = width // TILE
    quarter = psend.shape[3]
    quarters = psend.shape[0]

    def m4(v):
        return lax.rem(v, SIDE)

    def device(a_to, b_to):
        x_to = a_to * (1 - k) + b_to * k
        y_to = b_to * (1 - k) + a_to * k
        return (((l * SIDE + y_to) * SIDE + x_to) * 2 + k, p)

    def flat(h, a_at, b_at):
        return (a_at * (1 - h) + b_at * h) + SIDE * (b_at * (1 - h) + a_at * h)

    sibling = (fs + 1 - 2 * k, p)
    across = (fs + (1 - 2 * l) * (2 * SIDE * SIDE), p)
    a_next, a_prev, a_far = (device(m4(a + i), b) for i in (1, 3, 2))
    b_next, b_prev = device(a, m4(b + 1)), device(a, m4(b + 3))
    p_next, p_prev, p_far = m4(p + 1), m4(p + 3), m4(p + 2)
    dp_next, dp_prev = (fs, p_next), (fs, p_prev)

    sends = []

    def push(src, dst, recv_sem, to):
        copy = remote(src, dst, send_sem.at[len(sends)], recv_sem, to)
        sends.append(copy)
        copy.start()

    def arrive(dst, recv_sem):
        remote(dst, dst, send_sem.at[0], recv_sem, sibling).wait_recv()

    load_x = pltpu.make_async_copy(x_hbm.at[0], xall.at[p], local_sem.at[0])
    load_x.start()
    load_g = pltpu.make_async_copy(gt_hbm, gt.at[:, pl.ds(0, units), :], local_sem.at[1])
    load_g.start()

    barrier = pltpu.get_barrier_semaphore()
    peers = (sibling, across, a_next, a_prev, a_far, b_next, b_prev, dp_next, dp_prev)
    for peer in peers:
        pl.semaphore_signal(barrier, inc=1, device_id=place(peer), device_id_type=MESH)

    wst[k] = jnp.zeros(wst.shape[1:], F32)
    wst[k, :, pl.ds(0, units)] = w_ref[...].astype(F32)
    gt[:, pl.ds(units, width - units), :] = jnp.zeros((SIDE, width - units, toks), BF16)
    load_x.wait()
    pl.semaphore_wait(barrier, len(peers))

    mine = flat(k, a, b)

    def wblock(h, at):
        return wfull.at[h, at]

    def wsem(h, at):
        return w_sem.at[h * (SIDE * SIDE) + at]

    stage = remote(wst.at[k], wst.at[k], send_sem.at[send_sem.shape[0] - 1], s_sem.at[4], sibling)

    @pl.when(jnp.logical_not(home))
    def _():
        stage.start()

    lo, hi = pl.ds(0, half_toks), pl.ds(half_toks, half_toks)
    push(xall.at[p, lo], xall.at[p, lo], x_sem.at[0], dp_next)
    push(xall.at[p, hi], xall.at[p, hi], x_sem.at[2], dp_prev)
    push(xall.at[p, hi], xall.at[p, hi], x_sem.at[1], dp_next)
    push(xall.at[p, lo], xall.at[p, lo], x_sem.at[3], dp_prev)

    cross = remote(
        wblock(k, mine), wblock(k, mine), send_sem.at[send_sem.shape[0] - 2], wsem(k, mine), across
    )

    @pl.when(home)
    def _():
        arrive(wst.at[1 - k], s_sem.at[4])
        wfull[k, mine] = wst[...].reshape(rows, width).astype(BF16)
        cross.start()

    @pl.when(jnp.logical_not(home))
    def _():
        arrive(wblock(k, mine), wsem(k, mine))

    def share(at, *devices):
        for to in devices:
            push(wblock(k, at), wblock(k, at), wsem(k, at), to)

    order = (0, 1, 3, 2)
    by_next = (0, 3)
    share(mine, a_next, a_prev, a_far, b_next, b_prev, sibling)
    for i in order[1:]:
        at = flat(k, m4(a + i), b)
        arrive(wblock(k, at), wsem(k, at))
        share(at, b_next, b_prev, sibling)

    arrive(xall.at[p_prev, lo], x_sem.at[0])
    push(xall.at[p_prev, lo], xall.at[p_prev, lo], x_sem.at[4], dp_next)
    arrive(xall.at[p_next, hi], x_sem.at[2])
    push(xall.at[p_next, hi], xall.at[p_next, hi], x_sem.at[5], dp_prev)

    load_g.wait()

    def turn_g(step, _):
        clip, j = lax.div(step, tiles), lax.rem(step, tiles)
        at = pl.ds(pl.multiple_of(j * TILE, TILE), TILE)
        block = gt[clip, at, :].astype(F32).T.astype(BF16)
        g[pl.ds(pl.multiple_of(clip * toks, toks), toks), at] = block
        return 0

    lax.fori_loop(0, SIDE * tiles, turn_g, 0)

    for i in order:
        at = flat(k, m4(a + i), m4(b + 3))
        arrive(wblock(k, at), wsem(k, at))
        share(at, *((b_next, sibling) if i in by_next else (sibling,)))
        at = flat(k, m4(a + i), m4(b + 1))
        arrive(wblock(k, at), wsem(k, at))
        share(at, *((sibling,) if i in by_next else (b_prev, sibling)))
    for i in order:
        at = flat(k, m4(a + i), m4(b + 2))
        arrive(wblock(k, at), wsem(k, at))
        share(at, sibling)
    for at in range(SIDE * SIDE):
        arrive(wblock(1 - k, at), wsem(1 - k, at))
    arrive(xall.at[p_prev, hi], x_sem.at[1])
    arrive(xall.at[p_next, lo], x_sem.at[3])
    arrive(xall.at[p_far, lo], x_sem.at[4])
    arrive(xall.at[p_far, hi], x_sem.at[5])

    def forward(j, _):
        at = pl.ds(pl.multiple_of(j * TILE, TILE), TILE)
        pre[...] = jnp.dot(
            xall[...].reshape(SIDE * toks, -1), wfull[:, :, :, at].reshape(-1, TILE), preferred_element_type=F32
        )

        def chunk(r, _):
            span = pl.ds(pl.multiple_of(r * CHUNK, CHUNK), CHUNK)
            value, slope = gelu_pair(pre[span, :])
            outn[span, at] = value.astype(BF16)
            pg[span, at] = (g[span, at].astype(F32) * slope).astype(BF16)
            return 0

        lax.fori_loop(0, SIDE * toks // CHUNK, chunk, 0)
        return 0

    lax.fori_loop(0, tiles, forward, 0)

    blocks = quarter // rows
    for q in range(quarters):
        first = q * blocks
        h, at = first // (SIDE * SIDE), first % (SIDE * SIDE)
        wq = wfull[h, pl.ds(at, blocks)].reshape(quarter, width)
        part = lax.dot_general(pg[...], wq, (((1,), (1,)), ((), ())), preferred_element_type=F32)
        psend[q] = part.astype(BF16).reshape(SIDE, toks, quarter)
        push(psend.at[q, p_far, lo], zr1.at[q, 0], z1_sem.at[2 * q], dp_next)
        push(psend.at[q, p_far, hi], zr1.at[q, 1], z1_sem.at[2 * q + 1], dp_prev)

    def merge(q):
        arrive(zr1.at[q, 0], z1_sem.at[2 * q])
        psend[q, p_next, lo] = (psend[q, p_next, lo].astype(F32) + zr1[q, 0].astype(F32)).astype(BF16)
        push(psend.at[q, p_next], zr2.at[q, 0], z2_sem.at[2 * q], dp_next)
        arrive(zr1.at[q, 1], z1_sem.at[2 * q + 1])
        psend[q, p_prev, hi] = (psend[q, p_prev, hi].astype(F32) + zr1[q, 1].astype(F32)).astype(BF16)
        push(psend.at[q, p_prev], zr2.at[q, 1], z2_sem.at[2 * q + 1], dp_prev)

    def turn_x(clip, _):
        at = pl.ds(pl.multiple_of(clip * toks, toks), toks)
        for q in range(quarters):
            first = q * blocks
            h, here = first // (SIDE * SIDE), first % (SIDE * SIDE)
            block = xall[clip, :, pl.ds(q * quarter, quarter)].astype(F32).T.astype(BF16)
            xt[h, pl.ds(here, blocks), :, at] = block.reshape(blocks, rows, toks)
        return 0

    lax.fori_loop(0, SIDE, turn_x, 0)

    def slab(h, s, store):
        for i in range(SIDE):
            lhs[pl.ds(i * rows, rows), :] = xt[h, flat(h, i, s)]

        def step(j, _):
            at = pl.ds(pl.multiple_of(j * TILE, TILE), TILE)
            store(at, jnp.dot(lhs[...], pg[:, at], preferred_element_type=F32).reshape(SIDE, rows, TILE))
            return 0

        lax.fori_loop(0, tiles, step, 0)

    for n, i in enumerate((2, 1, 3, 0)):
        s = m4(a + i)

        def to_sibling(at, value):
            ssend[s, :, :, at] = value.astype(BF16)

        slab(1 - k, s, to_sibling)
        push(ssend.at[s], srecv.at[s], s_sem.at[n], sibling)
        merge(n)

    for n, i in enumerate((2, 1, 3, 0)):
        s = m4(b + i)
        arrive(srecv.at[s], s_sem.at[n])
        if i == 1:
            arrive(r1.at[0], r_sem.at[0])
        if i == 3:
            arrive(r1.at[1], r_sem.at[1])

        def keep(at, value):
            total = value + srecv[s, :, :, at].astype(F32)
            if i == 1:
                total = jnp.concatenate([total[:2] + r1[0, :, :, at].astype(F32), total[2:]], axis=0)
            if i == 3:
                total = jnp.concatenate([total[:2], total[2:] + r1[1, :, :, at].astype(F32)], axis=0)
            dsend[s, :, :, at] = total.astype(BF16)

        slab(k, s, keep)
        if i == 2:
            push(dsend.at[s, pl.ds(0, 2)], r1.at[0], r_sem.at[0], b_next)
            push(dsend.at[s, pl.ds(2, 2)], r1.at[1], r_sem.at[1], b_prev)
        if i == 1:
            push(dsend.at[s], r2.at[0], r_sem.at[2], b_next)
        if i == 3:
            push(dsend.at[s], r2.at[1], r_sem.at[3], b_prev)

    def turn_out(step, _):
        clip, j = lax.div(step, tiles), lax.rem(step, tiles)
        at = pl.ds(pl.multiple_of(j * TILE, TILE), TILE)
        block = outn[pl.ds(pl.multiple_of(clip * toks, toks), toks), at].astype(F32).T.astype(BF16)
        outt[clip, at, :] = block
        return 0

    lax.fori_loop(0, SIDE * tiles, turn_out, 0)
    store_out = pltpu.make_async_copy(outt.at[:, pl.ds(0, units), :], out_hbm, local_sem.at[1])
    store_out.start()

    arrive(r2.at[0], r_sem.at[2])
    arrive(r2.at[1], r_sem.at[3])
    for i, to in ((2, a_far), (1, a_next), (3, a_prev), (0, None)):
        ai = m4(a + i)

        def gathered(j, _):
            at = pl.ds(pl.multiple_of(j * TILE, TILE), TILE)
            total = dsend[b, ai, :, at].astype(F32) + r2[0, ai, :, at].astype(F32) + r2[1, ai, :, at].astype(F32)
            dsend[b, ai, :, at] = total.astype(BF16)
            return 0

        lax.fori_loop(0, tiles, gathered, 0)
        if to is not None:
            push(dsend.at[b, ai], r3.at[i - 1], r_sem.at[3 + i], to)

    for q in range(quarters):
        arrive(zr2.at[q, 0], z2_sem.at[2 * q])
        arrive(zr2.at[q, 1], z2_sem.at[2 * q + 1])
        total = psend[q, p].astype(F32) + zr2[q, 0].astype(F32) + zr2[q, 1].astype(F32)
        ing[:, pl.ds(q * quarter, quarter)] = total.astype(BF16)
    store_ing = pltpu.make_async_copy(ing, ing_hbm.at[0], local_sem.at[0])
    store_ing.start()

    for i in (1, 2, 3):
        arrive(r3.at[i - 1], r_sem.at[3 + i])

    def plane(at):
        return dsend[b, a, :, at].astype(F32) + sum(r3[i, :, at].astype(F32) for i in range(3))

    last = remote(d4, r4, send_sem.at[send_sem.shape[0] - 3], r_sem.at[7], across)
    back = remote(fin.at[1 - k], fin.at[1 - k], send_sem.at[send_sem.shape[0] - 4], s_sem.at[5], sibling)

    @pl.when(jnp.logical_not(home))
    def _():
        def step(j, _):
            at = pl.ds(pl.multiple_of(j * TILE, TILE), TILE)
            d4[:, at] = plane(at).astype(BF16)
            return 0

        lax.fori_loop(0, tiles, step, 0)
        last.start()
        last.wait_send()
        arrive(fin.at[k], s_sem.at[5])

    @pl.when(home)
    def _():
        arrive(r4, r_sem.at[7])

        def step(j, _):
            at = pl.ds(pl.multiple_of(j * TILE, TILE), TILE)
            fin[:, :, at] = ((plane(at) + r4[:, at].astype(F32)) * factor).reshape(2, rows // 2, TILE)
            return 0

        lax.fori_loop(0, tiles, step, 0)
        back.start()
        back.wait_send()

    dw_ref[...] = fin[k, :, pl.ds(0, units)]

    @pl.when(home)
    def _():
        cross.wait_send()

    @pl.when(jnp.logical_not(home))
    def _():
        stage.wait_send()

    for copy in sends:
        copy.wait_send()
    store_out.wait()
    store_ing.wait()


def on_device(inputs, up_weight, out_grad):
    _, toks, depth = inputs.shape
    own_rows, units = up_weight.shape
    clips = out_grad.shape[0]
    rows = 2 * own_rows
    chips = SIDE * SIDE
    width = -(-units // TILE) * TILE
    quarters = 4
    quarter = depth // quarters
    every = clips * toks
    factor = 1.0 / float(every * 4 * chips) ** 0.5

    out_t, in_grad, up_grad = pl.pallas_call(
        functools.partial(kernel, factor),
        out_shape=(
            jax.ShapeDtypeStruct((clips, units, toks), BF16),
            jax.ShapeDtypeStruct((1, toks, depth), BF16),
            jax.ShapeDtypeStruct((own_rows, units), F32),
        ),
        in_specs=[
            pl.BlockSpec(memory_space=pl.ANY),
            pl.BlockSpec(memory_space=pltpu.VMEM),
            pl.BlockSpec(memory_space=pl.ANY),
        ],
        out_specs=(
            pl.BlockSpec(memory_space=pl.ANY),
            pl.BlockSpec(memory_space=pl.ANY),
            pl.BlockSpec(memory_space=pltpu.VMEM),
        ),
        scratch_shapes=[
            pltpu.VMEM((clips, toks, depth), BF16),
            pltpu.VMEM((2, chips, rows, every), BF16),
            pltpu.VMEM((2, chips, rows, width), BF16),
            pltpu.VMEM((2, own_rows, width), F32),
            pltpu.VMEM((clips, width, toks), BF16),
            pltpu.VMEM((every, width), BF16),
            pltpu.VMEM((every, width), BF16),
            pltpu.VMEM((every, width), BF16),
            pltpu.VMEM((clips, width, toks), BF16),
            pltpu.VMEM((every, TILE), F32),
            pltpu.VMEM((quarters, clips, toks, quarter), BF16),
            pltpu.VMEM((quarters, 2, toks // 2, quarter), BF16),
            pltpu.VMEM((quarters, 2, toks, quarter), BF16),
            pltpu.VMEM((toks, depth), BF16),
            pltpu.VMEM((SIDE * rows, every), BF16),
            pltpu.VMEM((SIDE, SIDE, rows, width), BF16),
            pltpu.VMEM((SIDE, SIDE, rows, width), BF16),
            pltpu.VMEM((SIDE, SIDE, rows, width), BF16),
            pltpu.VMEM((2, 2, rows, width), BF16),
            pltpu.VMEM((2, SIDE, rows, width), BF16),
            pltpu.VMEM((3, rows, width), BF16),
            pltpu.VMEM((rows, width), BF16),
            pltpu.VMEM((rows, width), BF16),
            pltpu.VMEM((2, own_rows, width), F32),
            pltpu.SemaphoreType.DMA((72,)),
            pltpu.SemaphoreType.DMA((2 * chips,)),
            pltpu.SemaphoreType.DMA((6,)),
            pltpu.SemaphoreType.DMA((2 * quarters,)),
            pltpu.SemaphoreType.DMA((2 * quarters,)),
            pltpu.SemaphoreType.DMA((6,)),
            pltpu.SemaphoreType.DMA((8,)),
            pltpu.SemaphoreType.DMA((2,)),
        ],
        compiler_params=pltpu.CompilerParams(
            collective_id=0, has_side_effects=True, vmem_limit_bytes=60 * 1024 * 1024
        ),
        cost_estimate=pl.CostEstimate(
            flops=6 * every * depth * units, bytes_accessed=6_000_000, transcendentals=every * units
        ),
    )(inputs, up_weight, out_grad.transpose(0, 2, 1))
    return out_t.transpose(0, 2, 1), in_grad, up_grad


def solution(mesh):
    in_specs = (P("dp", "fsdp", None), P("fsdp", "dp"), P(None, "fsdp", "dp"))
    out_specs = (P(None, "fsdp", "dp"), P("dp", "fsdp", None), P("fsdp", "dp"))
    return jax.shard_map(
        on_device, mesh=mesh, in_specs=in_specs, out_specs=out_specs, check_vma=False
    )
```

time: 591 us -> 165 us (0.28)
  waiting for transfers between devices: 522 us -> 0 us
  Pallas kernels: 0 us -> 159 us
  matrix products: 29.3 us -> 0 us
  local copies, waits for them, and re-layouts: 20.6 us -> 4.43 us
  between operations: 13.8 us -> 0.66 us
    unnamed x5 -> x0, waiting for transfers between devices: 314 us -> none
    all_gather x2 -> x0, waiting for transfers between devices: 181 us -> none  [the longest x1 116 us: on_device(): up_whole = lax.all_gather(up_weight, 'fsdp', axis=0, tiled=True)]
    pallas_call x0 -> x1, Pallas kernels: none -> 159 us  [on_device(): pl.pallas_call(functools.partial(kernel, factor), out_shape=(jax.ShapeDty...]
    dot_general x3 -> x0, matrix products: 29.3 us -> none  [the longest x1 12.4 us: on_device(): pre = jnp.dot(tok_rows, up_whole, preferred_element_type=jnp.float32)]
    reduce_scatter x1 -> x0, waiting for transfers between devices: 26.5 us -> none  [on_device(): lax.psum_scatter(partial_rows.astype(jnp.bfloat16), 'dp', scatter_dimensi...]
    unnamed x3 -> x7, local copies, waits for them, and re-layouts: 19.1 us -> 4.43 us
  transfers between devices with their start and end apart: 4 -> 0, of which waited for: 4 -> 0; matrix products, arithmetic and copies ran while one was open for 5% -> 0% of each run, Pallas kernels for 0% -> 0%
where the time goes in v1:
time: 165 us
  Pallas kernels  159 us (96%)
  local copies, waits for them, and re-layouts  4.43 us (3%)
    pallas_call x1, Pallas kernels, on_device(): pl.pallas_call(functools.partial(kernel, factor), out_shape=(jax.ShapeDty...  159 us
    unnamed x7, local copies, waits for them, and re-layouts  4.43 us

profile of v1, /device:TPU:1, one launch (start us, length us, event | category | flops | bytes accessed | tf_op | source)
XLA Modules:
  0.0 164.5 jit_solution(15807931626798752503)
XLA Ops:
  0.6 159.5 %shard_map.58 = (bf16[4,1728,128]{2,1,0:T(8,128)(2,1)}, bf16[1,128,2560]{2,1,0:T(8,128)(2,1)}, f32[40,1728]{1,0:T(8,128)}) custom-call(bf16[1,128,2560]{2,1,0:T(8,128)(2,1)} %x_hbm.1, bf16[40,1728]{1,0:T(8,128)(2,1)} %w_ref.1, bf16[4,1728,128]{2,1,0:T(8,128)(2,1)} %bitcast.3), custom_call_target="tpu_custom_call" | custom-call | flops 13589544960 | bytes 6000000 | tf_op jit(solution)/shard_map/pallas_call | solution.py:373
  160.1 0.0 copy-start
  160.1 0.0 copy-start.1
  160.1 2.9 %copy.9 = bf16[4,128,1728]{1,2,0:T(8,128)(2,1)} copy(bf16[4,128,1728]{1,2,0:T(8,128)(2,1)} %bitcast.2) | data formatting | bytes 3538944
  163.0 0.0 copy-done
  163.0 0.8 copy.10
  163.8 0.0 copy-done.1
  163.8 0.7 copy.11
Async XLA Ops:
  160.1 2.9 %copy-start = (bf16[1,128,2560]{2,1,0:T(8,128)(2,1)S(1)}, bf16[1,128,2560]{2,1,0:T(8,128)(2,1)}, u32[]{:S(2)}) copy-start(bf16[1,128,2560]{2,1,0:T(8,128)(2,1)} %get-tuple-element.13) | copy-start | bytes 1966084
  160.1 3.7 %copy-start.1 = (f32[40,1728]{1,0:T(8,128)S(1)}, f32[40,1728]{1,0:T(8,128)}, u32[]{:S(2)}) copy-start(f32[40,1728]{1,0:T(8,128)} %get-tuple-element.14) | copy-start | bytes 829444

commit v2 on v1

v2 whole, which is shorter than its diff:
```python
import functools

import jax
import jax.numpy as jnp
from jax import lax
from jax.experimental import pallas as pl
from jax.experimental.pallas import tpu as pltpu
from jax.sharding import PartitionSpec as P

MESH = pl.DeviceIdType.MESH
F32, BF16 = jnp.float32, jnp.bfloat16
SIDE = 4
TILE = 256
CHUNK = 64


def place(device):
    return {"fsdp": device[0], "dp": device[1]}


def remote(src, dst, send_sem, recv_sem, device):
    return pltpu.make_async_remote_copy(
        src_ref=src, dst_ref=dst, send_sem=send_sem, recv_sem=recv_sem,
        device_id=place(device), device_id_type=MESH,
    )


def gelu_pair(v):
    c = 0.7978845608028654
    sq = v * v
    t = jnp.tanh(v * (c + (c * 0.044715) * sq))
    half = 0.5 * (1.0 + t)
    slope = half + (0.5 * v) * (1.0 - t * t) * (c + (3.0 * c * 0.044715) * sq)
    return v * half, slope


def kernel(
    factor, x_hbm, w_ref, gt_hbm, out_hbm, ing_hbm, dw_ref,
    xall, xt, wfull, wown, wst, gt, g, pg, outn, outt, pre, psend, zr1, zr2, ing,
    lhs, ssend, srecv, dsend, r1, r2, r3, d4, r4, fin,
    send_sem, w_sem, p_sem, x_sem, z1_sem, z2_sem, s_sem, r_sem, local_sem,
):
    fs, p = lax.axis_index("fsdp"), lax.axis_index("dp")
    k = lax.rem(fs, 2)
    x = lax.rem(lax.div(fs, 2), SIDE)
    y = lax.rem(lax.div(fs, 2 * SIDE), SIDE)
    l = lax.div(fs, 2 * SIDE * SIDE)
    home = k == l
    a = x * (1 - k) + y * k
    b = y * (1 - k) + x * k
    toks = xall.shape[1]
    half_toks = toks // 2
    near = (SIDE - 1) * toks
    rows = wfull.shape[2]
    own_rows = rows // 2
    width = wfull.shape[3]
    units = w_ref.shape[1]
    tiles = width // TILE
    quarter = psend.shape[3]
    quarters = psend.shape[0]
    blocks = quarter // rows

    def m4(v):
        return lax.rem(v, SIDE)

    def device(a_to, b_to):
        x_to = a_to * (1 - k) + b_to * k
        y_to = b_to * (1 - k) + a_to * k
        return (((l * SIDE + y_to) * SIDE + x_to) * 2 + k, p)

    def flat(h, a_at, b_at):
        return (a_at * (1 - h) + b_at * h) + SIDE * (b_at * (1 - h) + a_at * h)

    def clip_at(slot):
        return m4(p + jnp.where(slot == 0, 0, jnp.where(slot == 1, 3, slot - 1)))

    sibling = (fs + 1 - 2 * k, p)
    across = (fs + (1 - 2 * l) * (2 * SIDE * SIDE), p)
    askew = (across[0] + 1 - 2 * k, p)
    a_next, a_prev, a_far = (device(m4(a + i), b) for i in (1, 3, 2))
    b_next, b_prev = device(a, m4(b + 1)), device(a, m4(b + 3))
    dp_next, dp_prev = (fs, m4(p + 1)), (fs, m4(p + 3))

    sends = []

    def push(src, dst, recv_sem, to):
        copy = remote(src, dst, send_sem.at[len(sends)], recv_sem, to)
        sends.append(copy)
        copy.start()

    def arrive(dst, recv_sem):
        remote(dst, dst, send_sem.at[0], recv_sem, sibling).wait_recv()

    load_x = pltpu.make_async_copy(x_hbm.at[0], xall.at[0], local_sem.at[0])
    load_x.start()
    load_g = pltpu.make_async_copy(gt_hbm, gt.at[:, pl.ds(0, units), :], local_sem.at[1])
    load_g.start()

    barrier = pltpu.get_barrier_semaphore()
    peers = (sibling, across, askew, a_next, a_prev, a_far, b_next, b_prev, dp_next, dp_prev)
    for peer in peers:
        pl.semaphore_signal(barrier, inc=1, device_id=place(peer), device_id_type=MESH)

    spare = wown.shape[0] - own_rows
    wown[:, pl.ds(units, width - units)] = jnp.zeros((wown.shape[0], width - units), BF16)
    wown[:, pl.ds(0, units)] = jnp.concatenate([w_ref[...].astype(F32), jnp.zeros((spare, units), F32)], axis=0).astype(BF16)

    @pl.when(home)
    def _():
        wst[k] = wown[...]

    gt[:, pl.ds(units, width - units), :] = jnp.zeros((SIDE, width - units, toks), BF16)
    load_x.wait()
    pl.semaphore_wait(barrier, len(peers))

    mine = flat(k, a, b)

    def wblock(h, at):
        return wfull.at[h, at]

    def wsem(h, at):
        return w_sem.at[h * (SIDE * SIDE) + at]

    stage = remote(wown, wst.at[k], send_sem.at[send_sem.shape[0] - 1], p_sem.at[k], sibling)
    cross = remote(wown, wst.at[k], send_sem.at[send_sem.shape[0] - 2], p_sem.at[k], (across[0] + l - k, p))
    cross.start()

    @pl.when(jnp.logical_not(home))
    def _():
        stage.start()

    lo, hi = pl.ds(0, half_toks), pl.ds(half_toks, half_toks)
    push(xall.at[0, lo], xall.at[1, lo], x_sem.at[0], dp_next)
    push(xall.at[0, hi], xall.at[2, hi], x_sem.at[2], dp_prev)

    arrive(wst.at[1 - k], p_sem.at[1 - k])

    @pl.when(jnp.logical_not(home))
    def _():
        arrive(wst.at[k], p_sem.at[k])

    wfull[k, mine] = wst[...].astype(F32)[:, :own_rows].reshape(rows, width).astype(BF16)

    def share(at, *devices):
        for to in devices:
            push(wblock(k, at), wblock(k, at), wsem(k, at), to)

    order = (0, 1, 3, 2)
    by_next = (0, 3)
    share(mine, a_next, a_prev, a_far, b_next, b_prev, sibling)

    load_g.wait()

    def turn_g(step, _):
        slot, j = lax.div(step, tiles), lax.rem(step, tiles)
        at = pl.ds(pl.multiple_of(j * TILE, TILE), TILE)
        block = gt[clip_at(slot), at, :].astype(F32).T.astype(BF16)
        g[pl.ds(pl.multiple_of(slot * toks, toks), toks), at] = block
        return 0

    lax.fori_loop(0, SIDE * tiles, turn_g, 0)

    push(xall.at[0, hi], xall.at[1, hi], x_sem.at[1], dp_next)
    push(xall.at[0, lo], xall.at[2, lo], x_sem.at[3], dp_prev)
    for i in order[1:]:
        at = flat(k, m4(a + i), b)
        arrive(wblock(k, at), wsem(k, at))
        share(at, b_next, b_prev, sibling)

    arrive(xall.at[1, lo], x_sem.at[0])
    push(xall.at[1, lo], xall.at[3, lo], x_sem.at[4], dp_next)
    arrive(xall.at[2, hi], x_sem.at[2])
    push(xall.at[2, hi], xall.at[3, hi], x_sem.at[5], dp_prev)

    for i in order:
        at = flat(k, m4(a + i), m4(b + 3))
        arrive(wblock(k, at), wsem(k, at))
        share(at, *((b_next, sibling) if i in by_next else (sibling,)))
        at = flat(k, m4(a + i), m4(b + 1))
        arrive(wblock(k, at), wsem(k, at))
        share(at, *((sibling,) if i in by_next else (b_prev, sibling)))

    def turn_x(slot, _):
        at = pl.ds(pl.multiple_of(slot * toks, toks), toks)
        for q in range(quarters):
            first = q * blocks
            h, here = first // (SIDE * SIDE), first % (SIDE * SIDE)
            block = xall[slot, :, pl.ds(q * quarter, quarter)].astype(F32).T.astype(BF16)
            xt[h, pl.ds(here, blocks), :, at] = block.reshape(blocks, rows, toks)
        return 0

    arrive(xall.at[1, hi], x_sem.at[1])
    arrive(xall.at[2, lo], x_sem.at[3])
    lax.fori_loop(0, SIDE - 1, turn_x, 0)

    for i in order:
        at = flat(k, m4(a + i), m4(b + 2))
        arrive(wblock(k, at), wsem(k, at))
        share(at, sibling)
    for at in range(SIDE * SIDE):
        arrive(wblock(1 - k, at), wsem(1 - k, at))

    def forward(first, count):
        def tile(j, _):
            at = pl.ds(pl.multiple_of(j * TILE, TILE), TILE)
            pre[pl.ds(0, count * toks), :] = jnp.dot(
                xall[pl.ds(first, count)].reshape(count * toks, -1),
                wfull[:, :, :, at].reshape(-1, TILE), preferred_element_type=F32,
            )

            def chunk(r, _):
                span = pl.ds(pl.multiple_of(r * CHUNK, CHUNK), CHUNK)
                to = pl.ds(pl.multiple_of(r * CHUNK + first * toks, CHUNK), CHUNK)
                value, slope = gelu_pair(pre[span, :])
                outn[to, at] = value.astype(BF16)
                pg[to, at] = (g[to, at].astype(F32) * slope).astype(BF16)
                return 0

            lax.fori_loop(0, count * toks // CHUNK, chunk, 0)
            return 0

        lax.fori_loop(0, tiles, tile, 0)

    def in_grad_part(q, first, count):
        start = q * blocks
        h, at = start // (SIDE * SIDE), start % (SIDE * SIDE)
        wq = wfull[h, pl.ds(at, blocks)].reshape(quarter, width)
        part = lax.dot_general(
            pg[pl.ds(first * toks, count * toks), :], wq, (((1,), (1,)), ((), ())), preferred_element_type=F32
        )
        psend[q, pl.ds(first, count)] = part.astype(BF16).reshape(count, toks, quarter)

    forward(0, SIDE - 1)

    for q in range(quarters):
        in_grad_part(q, 0, SIDE - 1)
        push(psend.at[q, 2, hi], zr2.at[q, 0, hi], z2_sem.at[4 * q], dp_next)
        push(psend.at[q, 1, lo], zr2.at[q, 1, lo], z2_sem.at[4 * q + 1], dp_prev)

    arrive(xall.at[3, lo], x_sem.at[4])
    arrive(xall.at[3, hi], x_sem.at[5])
    forward(SIDE - 1, 1)

    for q in range(quarters):
        in_grad_part(q, SIDE - 1, 1)
        push(psend.at[q, 3, lo], zr1.at[q, 0], z1_sem.at[2 * q], dp_next)
        push(psend.at[q, 3, hi], zr1.at[q, 1], z1_sem.at[2 * q + 1], dp_prev)
    turn_x(SIDE - 1, 0)

    def merge(q):
        arrive(zr1.at[q, 0], z1_sem.at[2 * q])
        psend[q, 2, lo] = (psend[q, 2, lo].astype(F32) + zr1[q, 0].astype(F32)).astype(BF16)
        push(psend.at[q, 2, lo], zr2.at[q, 0, lo], z2_sem.at[4 * q + 2], dp_next)
        arrive(zr1.at[q, 1], z1_sem.at[2 * q + 1])
        psend[q, 1, hi] = (psend[q, 1, hi].astype(F32) + zr1[q, 1].astype(F32)).astype(BF16)
        push(psend.at[q, 1, hi], zr2.at[q, 1, hi], z2_sem.at[4 * q + 3], dp_prev)

    def slab(h, s):
        for i in range(SIDE):
            lhs[pl.ds(i * rows, rows), :] = xt[h, flat(h, i, s)]
        return jnp.dot(lhs[...], pg[...], preferred_element_type=F32).reshape(SIDE, rows, width)

    for n, i in enumerate((2, 1, 3, 0)):
        s = m4(a + i)
        ssend[s] = slab(1 - k, s).astype(BF16)
        push(ssend.at[s], srecv.at[s], s_sem.at[n], sibling)

    one, two = pl.ds(0, 2), pl.ds(2, 2)
    for n, i in enumerate((2, 1, 3, 0)):
        s = m4(b + i)
        arrive(srecv.at[s], s_sem.at[n])
        dsend[s] = (slab(k, s) + srecv[s].astype(F32)).astype(BF16)
        if i == 2:
            push(dsend.at[s, one], r1.at[0], r_sem.at[0], b_next)
            push(dsend.at[s, two], r1.at[1], r_sem.at[1], b_prev)
        if i == 1:
            push(dsend.at[s, two], r2.at[0, two], r_sem.at[2], b_next)
        if i == 3:
            push(dsend.at[s, one], r2.at[1, one], r_sem.at[3], b_prev)

    merge(0)
    s = m4(b + 1)
    arrive(r1.at[0], r_sem.at[0])
    dsend[s, one] = (dsend[s, one].astype(F32) + r1[0].astype(F32)).astype(BF16)
    push(dsend.at[s, one], r2.at[0, one], r_sem.at[8], b_next)
    s = m4(b + 3)
    arrive(r1.at[1], r_sem.at[1])
    dsend[s, two] = (dsend[s, two].astype(F32) + r1[1].astype(F32)).astype(BF16)
    push(dsend.at[s, two], r2.at[1, two], r_sem.at[9], b_prev)
    for q in range(1, quarters):
        merge(q)

    def turn_out(step, _):
        slot, j = lax.div(step, tiles), lax.rem(step, tiles)
        at = pl.ds(pl.multiple_of(j * TILE, TILE), TILE)
        block = outn[pl.ds(pl.multiple_of(slot * toks, toks), toks), at].astype(F32).T.astype(BF16)
        outt[clip_at(slot), at, :] = block
        return 0

    lax.fori_loop(0, SIDE * tiles, turn_out, 0)
    store_out = pltpu.make_async_copy(outt.at[:, pl.ds(0, units), :], out_hbm, local_sem.at[1])
    store_out.start()

    arrive(r2.at[0, two], r_sem.at[2])
    arrive(r2.at[1, one], r_sem.at[3])
    arrive(r2.at[0, one], r_sem.at[8])
    arrive(r2.at[1, two], r_sem.at[9])
    for i, to in ((2, a_far), (1, a_next), (3, a_prev), (0, None)):
        ai = m4(a + i)
        total = dsend[b, ai].astype(F32) + r2[0, ai].astype(F32) + r2[1, ai].astype(F32)
        dsend[b, ai] = total.astype(BF16)
        if to is not None:
            push(dsend.at[b, ai], r3.at[i - 1], r_sem.at[3 + i], to)

    for i in (1, 2, 3):
        arrive(r3.at[i - 1], r_sem.at[3 + i])

    def plane():
        return dsend[b, a].astype(F32) + r3[0].astype(F32) + r3[1].astype(F32) + r3[2].astype(F32)

    last = remote(d4, r4, send_sem.at[send_sem.shape[0] - 3], r_sem.at[7], across)
    back = remote(fin.at[1 - k], fin.at[1 - k], send_sem.at[send_sem.shape[0] - 4], s_sem.at[4], sibling)

    @pl.when(jnp.logical_not(home))
    def _():
        d4[...] = plane().astype(BF16)
        last.start()

    for q in range(quarters):
        arrive(zr2.at[q, 0, hi], z2_sem.at[4 * q])
        arrive(zr2.at[q, 1, lo], z2_sem.at[4 * q + 1])
        arrive(zr2.at[q, 0, lo], z2_sem.at[4 * q + 2])
        arrive(zr2.at[q, 1, hi], z2_sem.at[4 * q + 3])
        total = psend[q, 0].astype(F32) + zr2[q, 0].astype(F32) + zr2[q, 1].astype(F32)
        ing[:, pl.ds(q * quarter, quarter)] = total.astype(BF16)
    store_ing = pltpu.make_async_copy(ing, ing_hbm.at[0], local_sem.at[0])
    store_ing.start()

    @pl.when(home)
    def _():
        arrive(r4, r_sem.at[7])
        fin[...] = ((plane() + r4[...].astype(F32)) * factor).reshape(2, own_rows, width)
        back.start()
        back.wait_send()

    @pl.when(jnp.logical_not(home))
    def _():
        last.wait_send()
        arrive(fin.at[k], s_sem.at[4])

    dw_ref[...] = fin[k, :, pl.ds(0, units)]

    cross.wait_send()

    @pl.when(jnp.logical_not(home))
    def _():
        stage.wait_send()

    for copy in sends:
        copy.wait_send()
    store_out.wait()
    store_ing.wait()


def on_device(inputs, up_weight, out_grad):
    _, toks, depth = inputs.shape
    own_rows, units = up_weight.shape
    clips = out_grad.shape[0]
    rows = 2 * own_rows
    padded = -(-own_rows // 16) * 16
    chips = SIDE * SIDE
    width = -(-units // TILE) * TILE
    quarters = 4
    quarter = depth // quarters
    every = clips * toks
    factor = 1.0 / float(every * 4 * chips) ** 0.5

    out_t, in_grad, up_grad = pl.pallas_call(
        functools.partial(kernel, factor),
        out_shape=(
            jax.ShapeDtypeStruct((clips, units, toks), BF16),
            jax.ShapeDtypeStruct((1, toks, depth), BF16),
            jax.ShapeDtypeStruct((own_rows, units), F32),
        ),
        in_specs=[
            pl.BlockSpec(memory_space=pl.ANY),
            pl.BlockSpec(memory_space=pltpu.VMEM),
            pl.BlockSpec(memory_space=pl.ANY),
        ],
        out_specs=(
            pl.BlockSpec(memory_space=pl.ANY),
            pl.BlockSpec(memory_space=pl.ANY),
            pl.BlockSpec(memory_space=pltpu.VMEM),
        ),
        scratch_shapes=[
            pltpu.VMEM((clips, toks, depth), BF16),
            pltpu.VMEM((2, chips, rows, every), BF16),
            pltpu.VMEM((2, chips, rows, width), BF16),
            pltpu.VMEM((padded, width), BF16),
            pltpu.VMEM((2, padded, width), BF16),
            pltpu.VMEM((clips, width, toks), BF16),
            pltpu.VMEM((every, width), BF16),
            pltpu.VMEM((every, width), BF16),
            pltpu.VMEM((every, width), BF16),
            pltpu.VMEM((clips, width, toks), BF16),
            pltpu.VMEM((every, TILE), F32),
            pltpu.VMEM((quarters, clips, toks, quarter), BF16),
            pltpu.VMEM((quarters, 2, toks // 2, quarter), BF16),
            pltpu.VMEM((quarters, 2, toks, quarter), BF16),
            pltpu.VMEM((toks, depth), BF16),
            pltpu.VMEM((SIDE * rows, every), BF16),
            pltpu.VMEM((SIDE, SIDE, rows, width), BF16),
            pltpu.VMEM((SIDE, SIDE, rows, width), BF16),
            pltpu.VMEM((SIDE, SIDE, rows, width), BF16),
            pltpu.VMEM((2, 2, rows, width), BF16),
            pltpu.VMEM((2, SIDE, rows, width), BF16),
            pltpu.VMEM((3, rows, width), BF16),
            pltpu.VMEM((rows, width), BF16),
            pltpu.VMEM((rows, width), BF16),
            pltpu.VMEM((2, own_rows, width), F32),
            pltpu.SemaphoreType.DMA((96,)),
            pltpu.SemaphoreType.DMA((2 * chips,)),
            pltpu.SemaphoreType.DMA((2,)),
            pltpu.SemaphoreType.DMA((6,)),
            pltpu.SemaphoreType.DMA((2 * quarters,)),
            pltpu.SemaphoreType.DMA((4 * quarters,)),
            pltpu.SemaphoreType.DMA((6,)),
            pltpu.SemaphoreType.DMA((10,)),
            pltpu.SemaphoreType.DMA((2,)),
        ],
        compiler_params=pltpu.CompilerParams(
            collective_id=0, has_side_effects=True, vmem_limit_bytes=60 * 1024 * 1024
        ),
        cost_estimate=pl.CostEstimate(
            flops=6 * every * depth * units, bytes_accessed=6_000_000, transcendentals=every * units
        ),
    )(inputs, up_weight, out_grad.transpose(0, 2, 1))
    return out_t.transpose(0, 2, 1), in_grad, up_grad


def solution(mesh):
    in_specs = (P("dp", "fsdp", None), P("fsdp", "dp"), P(None, "fsdp", "dp"))
    out_specs = (P(None, "fsdp", "dp"), P("dp", "fsdp", None), P("fsdp", "dp"))
    return jax.shard_map(
        on_device, mesh=mesh, in_specs=in_specs, out_specs=out_specs, check_vma=False
    )
```

time: 165 us -> 130 us (0.79)
  Pallas kernels: 159 us -> 125 us
    pallas_call x1, Pallas kernels: 159 us -> 125 us  [on_device(): pl.pallas_call(functools.partial(kernel, factor), out_shape=(jax.ShapeDty...]
where the time goes in v2:
time: 130 us
  Pallas kernels  125 us (96%)
  local copies, waits for them, and re-layouts  4.43 us (3%)
    pallas_call x1, Pallas kernels, on_device(): pl.pallas_call(functools.partial(kernel, factor), out_shape=(jax.ShapeDty...  125 us
    unnamed x7, local copies, waits for them, and re-layouts  4.43 us

profile of v2, /device:TPU:1, one launch (start us, length us, event | category | flops | bytes accessed | tf_op | source)
XLA Modules:
  0.0 129.9 jit_solution(17299128968550963657)
XLA Ops:
  0.6 124.8 %shard_map.58 = (bf16[4,1728,128]{2,1,0:T(8,128)(2,1)}, bf16[1,128,2560]{2,1,0:T(8,128)(2,1)}, f32[40,1728]{1,0:T(8,128)}) custom-call(bf16[1,128,2560]{2,1,0:T(8,128)(2,1)} %x_hbm.1, bf16[40,1728]{1,0:T(8,128)(2,1)} %w_ref.1, bf16[4,1728,128]{2,1,0:T(8,128)(2,1)} %bitcast.3), custom_call_target="tpu_custom_call" | custom-call | flops 13589544960 | bytes 6000000 | tf_op jit(solution)/shard_map/pallas_call | solution.py:378
  125.5 0.0 copy-start
  125.5 0.0 copy-start.1
  125.5 2.9 %copy.9 = bf16[4,128,1728]{1,2,0:T(8,128)(2,1)} copy(bf16[4,128,1728]{1,2,0:T(8,128)(2,1)} %bitcast.2) | data formatting | bytes 3538944
  128.4 0.0 copy-done
  128.4 0.8 copy.10
  129.2 0.0 copy-done.1
  129.2 0.7 copy.11
Async XLA Ops:
  125.5 2.9 %copy-start = (bf16[1,128,2560]{2,1,0:T(8,128)(2,1)S(1)}, bf16[1,128,2560]{2,1,0:T(8,128)(2,1)}, u32[]{:S(2)}) copy-start(bf16[1,128,2560]{2,1,0:T(8,128)(2,1)} %get-tuple-element.13) | copy-start | bytes 1966084
  125.5 3.7 %copy-start.1 = (f32[40,1728]{1,0:T(8,128)S(1)}, f32[40,1728]{1,0:T(8,128)}, u32[]{:S(2)}) copy-start(f32[40,1728]{1,0:T(8,128)} %get-tuple-element.14) | copy-start | bytes 829444

commit v3 on v2

--- a/solution.py
+++ b/solution.py
@@ -37,7 +37,7 @@
 def kernel(
     factor, x_hbm, w_ref, gt_hbm, out_hbm, ing_hbm, dw_ref,
     xall, xt, wfull, wown, wst, gt, g, pg, outn, outt, pre, psend, zr1, zr2, ing,
-    lhs, ssend, srecv, dsend, r1, r2, r3, d4, r4, fin,
+    ssend, srecv, dsend, r1, r2, r3, d4, r4, fin,
     send_sem, w_sem, p_sem, x_sem, z1_sem, z2_sem, s_sem, r_sem, local_sem,
 ):
     fs, p = lax.axis_index("fsdp"), lax.axis_index("dp")
@@ -129,15 +129,15 @@
     def _():
         stage.start()
 
+    arrive(wst.at[1 - k], p_sem.at[1 - k])
+
+    @pl.when(jnp.logical_not(home))
+    def _():
+        arrive(wst.at[k], p_sem.at[k])
+
     lo, hi = pl.ds(0, half_toks), pl.ds(half_toks, half_toks)
     push(xall.at[0, lo], xall.at[1, lo], x_sem.at[0], dp_next)
     push(xall.at[0, hi], xall.at[2, hi], x_sem.at[2], dp_prev)
-
-    arrive(wst.at[1 - k], p_sem.at[1 - k])
-
-    @pl.when(jnp.logical_not(home))
-    def _():
-        arrive(wst.at[k], p_sem.at[k])
 
     wfull[k, mine] = wst[...].astype(F32)[:, :own_rows].reshape(rows, width).astype(BF16)
 
@@ -166,11 +166,6 @@
         at = flat(k, m4(a + i), b)
         arrive(wblock(k, at), wsem(k, at))
         share(at, b_next, b_prev, sibling)
-
-    arrive(xall.at[1, lo], x_sem.at[0])
-    push(xall.at[1, lo], xall.at[3, lo], x_sem.at[4], dp_next)
-    arrive(xall.at[2, hi], x_sem.at[2])
-    push(xall.at[2, hi], xall.at[3, hi], x_sem.at[5], dp_prev)
 
     for i in order:
         at = flat(k, m4(a + i), m4(b + 3))
@@ -180,27 +175,33 @@
         arrive(wblock(k, at), wsem(k, at))
         share(at, *((sibling,) if i in by_next else (b_prev, sibling)))
 
-    def turn_x(slot, _):
-        at = pl.ds(pl.multiple_of(slot * toks, toks), toks)
+    arrive(xall.at[1, lo], x_sem.at[0])
+    push(xall.at[1, lo], xall.at[3, lo], x_sem.at[4], dp_next)
+    arrive(xall.at[2, hi], x_sem.at[2])
+    push(xall.at[2, hi], xall.at[3, hi], x_sem.at[5], dp_prev)
+
+    def turn_x(slot):
+        at = pl.ds(slot * toks, toks)
         for q in range(quarters):
-            first = q * blocks
-            h, here = first // (SIDE * SIDE), first % (SIDE * SIDE)
-            block = xall[slot, :, pl.ds(q * quarter, quarter)].astype(F32).T.astype(BF16)
-            xt[h, pl.ds(here, blocks), :, at] = block.reshape(blocks, rows, toks)
-        return 0
-
-    arrive(xall.at[1, hi], x_sem.at[1])
-    arrive(xall.at[2, lo], x_sem.at[3])
-    lax.fori_loop(0, SIDE - 1, turn_x, 0)
+            block = xall[slot, :, pl.ds(q * quarter, quarter)].astype(F32).T.astype(BF16).reshape(blocks, rows, toks)
+            for i in range(blocks):
+                h, chip = divmod(q * blocks + i, SIDE * SIDE)
+                y_at, x_at = divmod(chip, SIDE)
+                first, second = (x_at, y_at) if h == 0 else (y_at, x_at)
+                xt[h, second, first, :, at] = block[i]
 
     for i in order:
         at = flat(k, m4(a + i), m4(b + 2))
         arrive(wblock(k, at), wsem(k, at))
         share(at, sibling)
+    arrive(xall.at[1, hi], x_sem.at[1])
+    arrive(xall.at[2, lo], x_sem.at[3])
+    for slot in range(SIDE - 1):
+        turn_x(slot)
     for at in range(SIDE * SIDE):
         arrive(wblock(1 - k, at), wsem(1 - k, at))
 
-    def forward(first, count):
+    def forward(first, count, start, stop):
         def tile(j, _):
             at = pl.ds(pl.multiple_of(j * TILE, TILE), TILE)
             pre[pl.ds(0, count * toks), :] = jnp.dot(
@@ -219,7 +220,7 @@
             lax.fori_loop(0, count * toks // CHUNK, chunk, 0)
             return 0
 
-        lax.fori_loop(0, tiles, tile, 0)
+        lax.fori_loop(start, stop, tile, 0)
 
     def in_grad_part(q, first, count):
         start = q * blocks
@@ -230,22 +231,76 @@
         )
         psend[q, pl.ds(first, count)] = part.astype(BF16).reshape(count, toks, quarter)
 
-    forward(0, SIDE - 1)
+    forward(0, SIDE - 1, 0, tiles)
 
     for q in range(quarters):
         in_grad_part(q, 0, SIDE - 1)
         push(psend.at[q, 2, hi], zr2.at[q, 0, hi], z2_sem.at[4 * q], dp_next)
         push(psend.at[q, 1, lo], zr2.at[q, 1, lo], z2_sem.at[4 * q + 1], dp_prev)
 
-    arrive(xall.at[3, lo], x_sem.at[4])
-    arrive(xall.at[3, hi], x_sem.at[5])
-    forward(SIDE - 1, 1)
-
-    for q in range(quarters):
-        in_grad_part(q, SIDE - 1, 1)
-        push(psend.at[q, 3, lo], zr1.at[q, 0], z1_sem.at[2 * q], dp_next)
-        push(psend.at[q, 3, hi], zr1.at[q, 1], z1_sem.at[2 * q + 1], dp_prev)
-    turn_x(SIDE - 1, 0)
+    one, two = pl.ds(0, 2), pl.ds(2, 2)
+    starts = [sum(d.shape[3] for d in dsend[:c]) for c in range(len(dsend))]
+
+    def slab(c, h, s):
+        at = pl.ds(starts[c], dsend[c].shape[3])
+        left = xt[h, s].reshape(SIDE * rows, SIDE * toks)
+        return jnp.dot(left, pg[:, at], preferred_element_type=F32).reshape(SIDE, rows, -1)
+
+    def slabs(c):
+        for n, i in enumerate((2, 1, 3, 0)):
+            s = m4(a + i)
+            ssend[c][s] = slab(c, 1 - k, s).astype(BF16)
+            push(ssend[c].at[s], srecv[c].at[s], s_sem.at[SIDE * c + n], sibling)
+        for n, i in enumerate((2, 1, 3, 0)):
+            s = m4(b + i)
+            arrive(srecv[c].at[s], s_sem.at[SIDE * c + n])
+            dsend[c][s] = (slab(c, k, s) + srecv[c][s].astype(F32)).astype(BF16)
+            if i == 2:
+                push(dsend[c].at[s, one], r1[c].at[0], r_sem.at[c, 0], b_next)
+                push(dsend[c].at[s, two], r1[c].at[1], r_sem.at[c, 1], b_prev)
+            if i == 1:
+                push(dsend[c].at[s, two], r2[c].at[0, two], r_sem.at[c, 2], b_next)
+            if i == 3:
+                push(dsend[c].at[s, one], r2[c].at[1, one], r_sem.at[c, 3], b_prev)
+
+    def pass_on(c):
+        s = m4(b + 1)
+        arrive(r1[c].at[0], r_sem.at[c, 0])
+        dsend[c][s, one] = (dsend[c][s, one].astype(F32) + r1[c][0].astype(F32)).astype(BF16)
+        push(dsend[c].at[s, one], r2[c].at[0, one], r_sem.at[c, 8], b_next)
+        s = m4(b + 3)
+        arrive(r1[c].at[1], r_sem.at[c, 1])
+        dsend[c][s, two] = (dsend[c][s, two].astype(F32) + r1[c][1].astype(F32)).astype(BF16)
+        push(dsend[c].at[s, two], r2[c].at[1, two], r_sem.at[c, 9], b_prev)
+
+    def along_first(c):
+        arrive(r2[c].at[0, two], r_sem.at[c, 2])
+        arrive(r2[c].at[1, one], r_sem.at[c, 3])
+        arrive(r2[c].at[0, one], r_sem.at[c, 8])
+        arrive(r2[c].at[1, two], r_sem.at[c, 9])
+        for i, to in ((2, a_far), (1, a_next), (3, a_prev), (0, None)):
+            ai = m4(a + i)
+            total = dsend[c][b, ai].astype(F32) + r2[c][0, ai].astype(F32) + r2[c][1, ai].astype(F32)
+            dsend[c][b, ai] = total.astype(BF16)
+            if to is not None:
+                push(dsend[c].at[b, ai], r3[c].at[i - 1], r_sem.at[c, 3 + i], to)
+
+    def plane(c):
+        return dsend[c][b, a].astype(F32) + r3[c][0].astype(F32) + r3[c][1].astype(F32) + r3[c][2].astype(F32)
+
+    last = [
+        remote(d4[c], r4[c], send_sem.at[send_sem.shape[0] - 4 - c], r_sem.at[c, 7], across) for c in range(len(d4))
+    ]
+    back = remote(fin.at[1 - k], fin.at[1 - k], send_sem.at[send_sem.shape[0] - 3], s_sem.at[s_sem.shape[0] - 1], sibling)
+
+    def across_planes(c):
+        for i in (1, 2, 3):
+            arrive(r3[c].at[i - 1], r_sem.at[c, 3 + i])
+
+        @pl.when(jnp.logical_not(home))
+        def _():
+            d4[c][...] = plane(c).astype(BF16)
+            last[c].start()
 
     def merge(q):
         arrive(zr1.at[q, 0], z1_sem.at[2 * q])
@@ -255,40 +310,27 @@
         psend[q, 1, hi] = (psend[q, 1, hi].astype(F32) + zr1[q, 1].astype(F32)).astype(BF16)
         push(psend.at[q, 1, hi], zr2.at[q, 1, hi], z2_sem.at[4 * q + 3], dp_prev)
 
-    def slab(h, s):
-        for i in range(SIDE):
-            lhs[pl.ds(i * rows, rows), :] = xt[h, flat(h, i, s)]
-        return jnp.dot(lhs[...], pg[...], preferred_element_type=F32).reshape(SIDE, rows, width)
-
-    for n, i in enumerate((2, 1, 3, 0)):
-        s = m4(a + i)
-        ssend[s] = slab(1 - k, s).astype(BF16)
-        push(ssend.at[s], srecv.at[s], s_sem.at[n], sibling)
-
-    one, two = pl.ds(0, 2), pl.ds(2, 2)
-    for n, i in enumerate((2, 1, 3, 0)):
-        s = m4(b + i)
-        arrive(srecv.at[s], s_sem.at[n])
-        dsend[s] = (slab(k, s) + srecv[s].astype(F32)).astype(BF16)
-        if i == 2:
-            push(dsend.at[s, one], r1.at[0], r_sem.at[0], b_next)
-            push(dsend.at[s, two], r1.at[1], r_sem.at[1], b_prev)
-        if i == 1:
-            push(dsend.at[s, two], r2.at[0, two], r_sem.at[2], b_next)
-        if i == 3:
-            push(dsend.at[s, one], r2.at[1, one], r_sem.at[3], b_prev)
-
+    arrive(xall.at[3, lo], x_sem.at[4])
+    arrive(xall.at[3, hi], x_sem.at[5])
+    turn_x(SIDE - 1)
+    forward(SIDE - 1, 1, 0, starts[1] // TILE)
+    slabs(0)
+    forward(SIDE - 1, 1, starts[1] // TILE, tiles)
+    pass_on(0)
+
+    for q in range(quarters):
+        in_grad_part(q, SIDE - 1, 1)
+        push(psend.at[q, 3, lo], zr1.at[q, 0], z1_sem.at[2 * q], dp_next)
+        push(psend.at[q, 3, hi], zr1.at[q, 1], z1_sem.at[2 * q + 1], dp_prev)
+
+    slabs(1)
+    along_first(0)
+    pass_on(1)
     merge(0)
-    s = m4(b + 1)
-    arrive(r1.at[0], r_sem.at[0])
-    dsend[s, one] = (dsend[s, one].astype(F32) + r1[0].astype(F32)).astype(BF16)
-    push(dsend.at[s, one], r2.at[0, one], r_sem.at[8], b_next)
-    s = m4(b + 3)
-    arrive(r1.at[1], r_sem.at[1])
-    dsend[s, two] = (dsend[s, two].astype(F32) + r1[1].astype(F32)).astype(BF16)
-    push(dsend.at[s, two], r2.at[1, two], r_sem.at[9], b_prev)
-    for q in range(1, quarters):
-        merge(q)
+    merge(1)
+    across_planes(0)
+    merge(2)
+    merge(3)
 
     def turn_out(step, _):
         slot, j = lax.div(step, tiles), lax.rem(step, tiles)
@@ -297,34 +339,11 @@
         outt[clip_at(slot), at, :] = block
         return 0
 
+    along_first(1)
     lax.fori_loop(0, SIDE * tiles, turn_out, 0)
     store_out = pltpu.make_async_copy(outt.at[:, pl.ds(0, units), :], out_hbm, local_sem.at[1])
     store_out.start()
-
-    arrive(r2.at[0, two], r_sem.at[2])
-    arrive(r2.at[1, one], r_sem.at[3])
-    arrive(r2.at[0, one], r_sem.at[8])
-    arrive(r2.at[1, two], r_sem.at[9])
-    for i, to in ((2, a_far), (1, a_next), (3, a_prev), (0, None)):
-        ai = m4(a + i)
-        total = dsend[b, ai].astype(F32) + r2[0, ai].astype(F32) + r2[1, ai].astype(F32)
-        dsend[b, ai] = total.astype(BF16)
-        if to is not None:
-            push(dsend.at[b, ai], r3.at[i - 1], r_sem.at[3 + i], to)
-
-    for i in (1, 2, 3):
-        arrive(r3.at[i - 1], r_sem.at[3 + i])
-
-    def plane():
-        return dsend[b, a].astype(F32) + r3[0].astype(F32) + r3[1].astype(F32) + r3[2].astype(F32)
-
-    last = remote(d4, r4, send_sem.at[send_sem.shape[0] - 3], r_sem.at[7], across)
-    back = remote(fin.at[1 - k], fin.at[1 - k], send_sem.at[send_sem.shape[0] - 4], s_sem.at[4], sibling)
-
-    @pl.when(jnp.logical_not(home))
-    def _():
-        d4[...] = plane().astype(BF16)
-        last.start()
+    across_planes(1)
 
     for q in range(quarters):
         arrive(zr2.at[q, 0, hi], z2_sem.at[4 * q])
@@ -338,15 +357,18 @@
 
     @pl.when(home)
     def _():
-        arrive(r4, r_sem.at[7])
-        fin[...] = ((plane() + r4[...].astype(F32)) * factor).reshape(2, own_rows, width)
+        for c in range(len(d4)):
+            arrive(r4[c], r_sem.at[c, 7])
+            whole = ((plane(c) + r4[c][...].astype(F32)) * factor).reshape(2, own_rows, -1)
+            fin[:, :, pl.ds(starts[c], d4[c].shape[1])] = whole
         back.start()
         back.wait_send()
 
     @pl.when(jnp.logical_not(home))
     def _():
-        last.wait_send()
-        arrive(fin.at[k], s_sem.at[4])
+        for copy in last:
+            copy.wait_send()
+        arrive(fin.at[k], s_sem.at[s_sem.shape[0] - 1])
 
     dw_ref[...] = fin[k, :, pl.ds(0, units)]
 
@@ -374,6 +396,11 @@
     quarter = depth // quarters
     every = clips * toks
     factor = 1.0 / float(every * 4 * chips) ** 0.5
+
+    first_chunk = width // TILE // 2 * TILE
+
+    def per_chunk(*lead):
+        return tuple(pltpu.VMEM((*lead, columns), BF16) for columns in (first_chunk, width - first_chunk))
 
     out_t, in_grad, up_grad = pl.pallas_call(
         functools.partial(kernel, factor),
@@ -394,7 +421,7 @@
         ),
         scratch_shapes=[
             pltpu.VMEM((clips, toks, depth), BF16),
-            pltpu.VMEM((2, chips, rows, every), BF16),
+            pltpu.VMEM((2, SIDE, SIDE, rows, every), BF16),
             pltpu.VMEM((2, chips, rows, width), BF16),
             pltpu.VMEM((padded, width), BF16),
             pltpu.VMEM((2, padded, width), BF16),
@@ -408,24 +435,23 @@
             pltpu.VMEM((quarters, 2, toks // 2, quarter), BF16),
             pltpu.VMEM((quarters, 2, toks, quarter), BF16),
             pltpu.VMEM((toks, depth), BF16),
-            pltpu.VMEM((SIDE * rows, every), BF16),
-            pltpu.VMEM((SIDE, SIDE, rows, width), BF16),
-            pltpu.VMEM((SIDE, SIDE, rows, width), BF16),
-            pltpu.VMEM((SIDE, SIDE, rows, width), BF16),
-            pltpu.VMEM((2, 2, rows, width), BF16),
-            pltpu.VMEM((2, SIDE, rows, width), BF16),
-            pltpu.VMEM((3, rows, width), BF16),
-            pltpu.VMEM((rows, width), BF16),
-            pltpu.VMEM((rows, width), BF16),
+            per_chunk(SIDE, SIDE, rows),
+            per_chunk(SIDE, SIDE, rows),
+            per_chunk(SIDE, SIDE, rows),
+            per_chunk(2, 2, rows),
+            per_chunk(2, SIDE, rows),
+            per_chunk(3, rows),
+            per_chunk(rows),
+            per_chunk(rows),
             pltpu.VMEM((2, own_rows, width), F32),
-            pltpu.SemaphoreType.DMA((96,)),
+            pltpu.SemaphoreType.DMA((112,)),
             pltpu.SemaphoreType.DMA((2 * chips,)),
             pltpu.SemaphoreType.DMA((2,)),
             pltpu.SemaphoreType.DMA((6,)),
             pltpu.SemaphoreType.DMA((2 * quarters,)),
             pltpu.SemaphoreType.DMA((4 * quarters,)),
-            pltpu.SemaphoreType.DMA((6,)),
-            pltpu.SemaphoreType.DMA((10,)),
+            pltpu.SemaphoreType.DMA((2 * SIDE + 1,)),
+            pltpu.SemaphoreType.DMA((2, 10)),
             pltpu.SemaphoreType.DMA((2,)),
         ],
         compiler_params=pltpu.CompilerParams(

time: 130 us -> 120 us (0.923)
  Pallas kernels: 125 us -> 115 us
    pallas_call x1, Pallas kernels: 125 us -> 115 us  [on_device(): pl.pallas_call(functools.partial(kernel, factor), out_shape=(jax.ShapeDty...]
where the time goes in v3:
time: 120 us
  Pallas kernels  115 us (96%)
  local copies, waits for them, and re-layouts  4.43 us (4%)
    pallas_call x1, Pallas kernels, on_device(): pl.pallas_call(functools.partial(kernel, factor), out_shape=(jax.ShapeDty...  115 us
    unnamed x7, local copies, waits for them, and re-layouts  4.43 us

profile of v3, /device:TPU:1, one launch (start us, length us, event | category | flops | bytes accessed | tf_op | source)
XLA Modules:
  0.0 119.8 jit_solution(354792739756042343)
XLA Ops:
  0.6 114.7 %shard_map.58 = (bf16[4,1728,128]{2,1,0:T(8,128)(2,1)}, bf16[1,128,2560]{2,1,0:T(8,128)(2,1)}, f32[40,1728]{1,0:T(8,128)}) custom-call(bf16[1,128,2560]{2,1,0:T(8,128)(2,1)} %x_hbm.1, bf16[40,1728]{1,0:T(8,128)(2,1)} %w_ref.1, bf16[4,1728,128]{2,1,0:T(8,128)(2,1)} %bitcast.3), custom_call_target="tpu_custom_call" | custom-call | flops 13589544960 | bytes 6000000 | tf_op jit(solution)/shard_map/pallas_call | solution.py:405
  115.4 0.0 copy-start
  115.4 0.0 copy-start.1
  115.4 2.9 %copy.9 = bf16[4,128,1728]{1,2,0:T(8,128)(2,1)} copy(bf16[4,128,1728]{1,2,0:T(8,128)(2,1)} %bitcast.2) | data formatting | bytes 3538944
  118.3 0.0 copy-done
  118.3 0.8 copy.10
  119.1 0.0 copy-done.1
  119.1 0.7 copy.11
Async XLA Ops:
  115.4 2.9 %copy-start = (bf16[1,128,2560]{2,1,0:T(8,128)(2,1)S(1)}, bf16[1,128,2560]{2,1,0:T(8,128)(2,1)}, u32[]{:S(2)}) copy-start(bf16[1,128,2560]{2,1,0:T(8,128)(2,1)} %get-tuple-element.13) | copy-start | bytes 1966084
  115.4 3.7 %copy-start.1 = (f32[40,1728]{1,0:T(8,128)S(1)}, f32[40,1728]{1,0:T(8,128)}, u32[]{:S(2)}) copy-start(f32[40,1728]{1,0:T(8,128)} %get-tuple-element.14) | copy-start | bytes 829444

commit v4 on v3

--- a/solution.py
+++ b/solution.py
@@ -202,25 +202,26 @@
         arrive(wblock(1 - k, at), wsem(1 - k, at))
 
     def forward(first, count, start, stop):
-        def tile(j, _):
-            at = pl.ds(pl.multiple_of(j * TILE, TILE), TILE)
-            pre[pl.ds(0, count * toks), :] = jnp.dot(
+        def product(j, slot):
+            at = pl.ds(j * TILE, TILE)
+            pre[slot, pl.ds(0, count * toks), :] = jnp.dot(
                 xall[pl.ds(first, count)].reshape(count * toks, -1),
                 wfull[:, :, :, at].reshape(-1, TILE), preferred_element_type=F32,
             )
 
-            def chunk(r, _):
-                span = pl.ds(pl.multiple_of(r * CHUNK, CHUNK), CHUNK)
-                to = pl.ds(pl.multiple_of(r * CHUNK + first * toks, CHUNK), CHUNK)
-                value, slope = gelu_pair(pre[span, :])
+        def activate(j, slot):
+            at = pl.ds(j * TILE, TILE)
+            for r in range(count * toks // CHUNK):
+                to = pl.ds(r * CHUNK + first * toks, CHUNK)
+                value, slope = gelu_pair(pre[slot, pl.ds(r * CHUNK, CHUNK), :])
                 outn[to, at] = value.astype(BF16)
                 pg[to, at] = (g[to, at].astype(F32) * slope).astype(BF16)
-                return 0
-
-            lax.fori_loop(0, count * toks // CHUNK, chunk, 0)
-            return 0
-
-        lax.fori_loop(start, stop, tile, 0)
+
+        for j in range(start, stop + 1):
+            if j > start:
+                activate(j - 1, (j - 1) % 2)
+            if j < stop:
+                product(j, j % 2)
 
     def in_grad_part(q, first, count):
         start = q * blocks
@@ -430,7 +431,7 @@
             pltpu.VMEM((every, width), BF16),
             pltpu.VMEM((every, width), BF16),
             pltpu.VMEM((clips, width, toks), BF16),
-            pltpu.VMEM((every, TILE), F32),
+            pltpu.VMEM((2, every, TILE), F32),
             pltpu.VMEM((quarters, clips, toks, quarter), BF16),
             pltpu.VMEM((quarters, 2, toks // 2, quarter), BF16),
             pltpu.VMEM((quarters, 2, toks, quarter), BF16),

time: 120 us -> 117 us (0.975)
  Pallas kernels: 115 us -> 112 us
    pallas_call x1, Pallas kernels: 115 us -> 112 us  [on_device(): pl.pallas_call(functools.partial(kernel, factor), out_shape=(jax.ShapeDty...]
where the time goes in v4:
time: 117 us
  Pallas kernels  112 us (96%)
  local copies, waits for them, and re-layouts  4.43 us (4%)
    pallas_call x1, Pallas kernels, on_device(): pl.pallas_call(functools.partial(kernel, factor), out_shape=(jax.ShapeDty...  112 us
    unnamed x7, local copies, waits for them, and re-layouts  4.43 us

profile of v4, /device:TPU:1, one launch (start us, length us, event | category | flops | bytes accessed | tf_op | source)
XLA Modules:
  0.0 116.6 jit_solution(10325906701667993039)
XLA Ops:
  0.6 111.5 %shard_map.58 = (bf16[4,1728,128]{2,1,0:T(8,128)(2,1)}, bf16[1,128,2560]{2,1,0:T(8,128)(2,1)}, f32[40,1728]{1,0:T(8,128)}) custom-call(bf16[1,128,2560]{2,1,0:T(8,128)(2,1)} %x_hbm.1, bf16[40,1728]{1,0:T(8,128)(2,1)} %w_ref.1, bf16[4,1728,128]{2,1,0:T(8,128)(2,1)} %bitcast.3), custom_call_target="tpu_custom_call" | custom-call | flops 13589544960 | bytes 6000000 | tf_op jit(solution)/shard_map/pallas_call | solution.py:406
  112.2 0.0 copy-start
  112.2 0.0 copy-start.1
  112.2 2.9 %copy.9 = bf16[4,128,1728]{1,2,0:T(8,128)(2,1)} copy(bf16[4,128,1728]{1,2,0:T(8,128)(2,1)} %bitcast.2) | data formatting | bytes 3538944
  115.1 0.0 copy-done
  115.1 0.8 copy.10
  115.9 0.0 copy-done.1
  115.9 0.7 copy.11
Async XLA Ops:
  112.2 2.9 %copy-start = (bf16[1,128,2560]{2,1,0:T(8,128)(2,1)S(1)}, bf16[1,128,2560]{2,1,0:T(8,128)(2,1)}, u32[]{:S(2)}) copy-start(bf16[1,128,2560]{2,1,0:T(8,128)(2,1)} %get-tuple-element.13) | copy-start | bytes 1966084
  112.2 3.7 %copy-start.1 = (f32[40,1728]{1,0:T(8,128)S(1)}, f32[40,1728]{1,0:T(8,128)}, u32[]{:S(2)}) copy-start(f32[40,1728]{1,0:T(8,128)} %get-tuple-element.14) | copy-start | bytes 829444

commit v5 on v4

--- a/solution.py
+++ b/solution.py
@@ -303,6 +303,10 @@
             d4[c][...] = plane(c).astype(BF16)
             last[c].start()
 
+        @pl.when(home)
+        def _():
+            fin[:, :, pl.ds(starts[c], d4[c].shape[1])] = plane(c).reshape(2, own_rows, -1)
+
     def merge(q):
         arrive(zr1.at[q, 0], z1_sem.at[2 * q])
         psend[q, 2, lo] = (psend[q, 2, lo].astype(F32) + zr1[q, 0].astype(F32)).astype(BF16)
@@ -360,8 +364,8 @@
     def _():
         for c in range(len(d4)):
             arrive(r4[c], r_sem.at[c, 7])
-            whole = ((plane(c) + r4[c][...].astype(F32)) * factor).reshape(2, own_rows, -1)
-            fin[:, :, pl.ds(starts[c], d4[c].shape[1])] = whole
+            at = pl.ds(starts[c], d4[c].shape[1])
+            fin[:, :, at] = (fin[:, :, at] + r4[c][...].astype(F32).reshape(2, own_rows, -1)) * factor
         back.start()
         back.wait_send()
 

time: 117 us -> 117 us (level)
  no operation moved by 1% of the time
where the time goes in v5:
time: 117 us
  Pallas kernels  112 us (96%)
  local copies, waits for them, and re-layouts  4.43 us (4%)
    pallas_call x1, Pallas kernels, on_device(): pl.pallas_call(functools.partial(kernel, factor), out_shape=(jax.ShapeDty...  112 us
    unnamed x7, local copies, waits for them, and re-layouts  4.43 us

profile of v5, /device:TPU:1, one launch (start us, length us, event | category | flops | bytes accessed | tf_op | source)
XLA Modules:
  0.0 116.6 jit_solution(12113540961144363228)
XLA Ops:
  0.6 111.5 %shard_map.58 = (bf16[4,1728,128]{2,1,0:T(8,128)(2,1)}, bf16[1,128,2560]{2,1,0:T(8,128)(2,1)}, f32[40,1728]{1,0:T(8,128)}) custom-call(bf16[1,128,2560]{2,1,0:T(8,128)(2,1)} %x_hbm.1, bf16[40,1728]{1,0:T(8,128)(2,1)} %w_ref.1, bf16[4,1728,128]{2,1,0:T(8,128)(2,1)} %bitcast.3), custom_call_target="tpu_custom_call" | custom-call | flops 13589544960 | bytes 6000000 | tf_op jit(solution)/shard_map/pallas_call | solution.py:410
  112.2 0.0 copy-start
  112.2 0.0 copy-start.1
  112.2 2.9 %copy.9 = bf16[4,128,1728]{1,2,0:T(8,128)(2,1)} copy(bf16[4,128,1728]{1,2,0:T(8,128)(2,1)} %bitcast.2) | data formatting | bytes 3538944
  115.1 0.0 copy-done
  115.1 0.8 copy.10
  115.9 0.0 copy-done.1
  115.9 0.7 copy.11
Async XLA Ops:
  112.2 2.9 %copy-start = (bf16[1,128,2560]{2,1,0:T(8,128)(2,1)S(1)}, bf16[1,128,2560]{2,1,0:T(8,128)(2,1)}, u32[]{:S(2)}) copy-start(bf16[1,128,2560]{2,1,0:T(8,128)(2,1)} %get-tuple-element.13) | copy-start | bytes 1966084
  112.2 3.7 %copy-start.1 = (f32[40,1728]{1,0:T(8,128)S(1)}, f32[40,1728]{1,0:T(8,128)}, u32[]{:S(2)}) copy-start(f32[40,1728]{1,0:T(8,128)} %get-tuple-element.14) | copy-start | bytes 829444
